TPU v7x, 32 devices: a whole 2x2x4 slice. The times are simulated.
32 devices in a mesh: gx: 8 (over z, x), gy: 4 (over y, core).
Axes of the slice: x: 2, y: 2, z: 4, core: 2. Of those that a mesh axis runs over, the one named last changes fastest.
Arguments:
- blocks: float32 [8, 4, 64, 4, 128], P('gx', 'gy'), may hold values from 0 to 1, as said below
- active_counts: int32 [8, 4], P('gx', 'gy'), may hold values from 1 to 32, as said below
- pair_lists: int32 [8, 4, 32, 16], P('gx', 'gy'), may hold values from 0 to 575
- cell_ids: int32 [8, 4, 64], P('gx', 'gy'), may hold values from 0 to 15, as said below
Outputs:
- accel: float32 [8, 4, 32, 3, 128], P('gx', 'gy')
Inputs may be any that keep to these rules, and one draw needn't show every extreme that they name: `active_counts`: every domain has at least one active block and some domain has 32; the active blocks are the first ones of the domain. `pair_lists`: entry (3 a + b) * 64 + n names block n of the domain a - 1 steps along gx and b - 1 steps along gy, with wrap around; a list may repeat a block or name the target block itself. `cell_ids`: A block of domain (i, j) lies in one of the 2 cells (g * 2 + h) with g = (i // 2) * (4 // 2) + j // 2. `blocks`: coordinates lie in [0, 1); masses are positive.
All inputs are finite; a program needn't handle non-finite values.
Results may differ from a plain program's by a relative error of at most 0.0003.
Values sent between devices are 32-bit elements; how exact they have to be, the bound alone decides.
No kernel may reach another device: no remote copies, remote signals or barrier semaphores. Data moves between devices by JAX's collectives and lax.ppermute only.
A program may use at most 64 MiB of HBM per device.

v0:
```python
import jax
import jax.numpy as jnp
from jax import lax
from jax.sharding import PartitionSpec as P

SUBC = 2


soft_near = 0.05
soft_far = 1.0


def padded_2(block, sides, width):
    for axis, dim in sides:
        count = lax.axis_size(axis)
        forward = [(i, i + 1) for i in range(count - 1)]
        forward.append((count - 1, 0))
        backward = [(target, source) for source, target in forward]
        low = lax.ppermute(
            lax.slice_in_dim(block, block.shape[dim] - width, None, axis=dim), axis, forward
        )
        high = lax.ppermute(lax.slice_in_dim(block, 0, width, axis=dim), axis, backward)
        block = jnp.concatenate([low, block, high], axis=dim)
    return block


def pair_accel(target, sources):
    offset = sources[:, :3, None, :] - target[None, :3, :, None]
    dist_sq = jnp.sum(offset * offset, axis=1) + soft_near * soft_near
    weight = sources[:, 3, None, :] * dist_sq ** (-1.5)
    return jnp.sum(weight[:, None, :, :] * offset, axis=(0, 3))


def far_accel(position, centres, cell_mass):
    offset = centres[:, None, :] - position[:, :, None]
    dist_sq = jnp.sum(offset * offset, axis=0) + soft_far * soft_far
    weight = cell_mass[None, :] * dist_sq ** (-1.5)
    return jnp.sum(weight[None, :, :] * offset, axis=2)


def cell_centres(total, half_gy):
    cell = jnp.arange(total, dtype=jnp.int32)
    group = cell // SUBC
    sub_cell = cell % SUBC
    centre_x = (2 * (group // half_gy) + 1).astype(jnp.float32)
    centre_y = (2 * (group % half_gy) + 1).astype(jnp.float32)
    centre_z = (sub_cell.astype(jnp.float32) + 0.5) / SUBC
    return jnp.stack([centre_x, centre_y, centre_z], axis=0)


def body(blocks, active_counts, pair_lists, cell_ids):
    count_blocks = blocks.shape[2]
    width = blocks.shape[4]
    slots = pair_lists.shape[2]
    total = lax.axis_size("gx") // 2 * (lax.axis_size("gy") // 2) * SUBC
    local = blocks[0, 0]
    block_mass = jnp.sum(local[:, 3, :], axis=-1)
    member = cell_ids[0, 0][:, None] == jnp.arange(total, dtype=jnp.int32)[None, :]
    partial_mass = jnp.sum(jnp.where(member, block_mass[:, None], 0.0), axis=0)
    cell_mass = lax.psum(partial_mass, ("gx", "gy"))
    centres = cell_centres(total, lax.axis_size("gy") // 2)
    padded = padded_2(blocks, (("gx", 0), ("gy", 1)), 1)
    steps = (jnp.arange(3, dtype=jnp.int32) - 1).astype(jnp.float32)
    zeros_grid = jnp.zeros((3, 3), jnp.float32)
    moved = jnp.stack(
        [steps[:, None] + zeros_grid, steps[None, :] + zeros_grid, zeros_grid, zeros_grid], axis=-1
    )
    table = (padded + moved[:, :, None, :, None]).reshape(9 * count_blocks, 4, width)
    corner = jnp.stack(
        [lax.axis_index("gx"), lax.axis_index("gy"), jnp.zeros((), jnp.int32)]
    ).astype(jnp.float32)[:, None]
    lists = pair_lists[0, 0]
    limit = active_counts[0, 0]

    def one_slot(slot_index):
        target = local[slot_index]
        near = pair_accel(target, table[lists[slot_index]])
        far = far_accel(target[:3] + corner, centres, cell_mass)
        return jnp.where(slot_index < limit, near + far, jnp.zeros_like(near))

    result = lax.map(one_slot, jnp.arange(slots, dtype=jnp.int32))
    return result[None, None]


def solution(mesh):
    in_specs = (
        P("gx", "gy", None, None, None),
        P("gx", "gy"),
        P("gx", "gy", None, None),
        P("gx", "gy", None),
    )
    out_specs = P("gx", "gy", None, None, None)
    return jax.shard_map(body, mesh=mesh, in_specs=in_specs, out_specs=out_specs, check_vma=False)
```

profile of v0, /device:TPU:0, one launch (start us, length us, event | category | flops | bytes accessed | tf_op | source)
XLA Modules:
  0.0 345.6 jit_solution(7272945098170407637)
XLA Ops:
  0.0 2.9 collective-permute-start
  2.9 3.0 collective-permute-start.1
  6.0 1.5 slice_reduce_fusion
  8.3 38.1 %psum.7 = f32[16]{0:T(128)S(1)} all-reduce(f32[16]{0:T(128)S(1)} %select_reduce_fusion), channel_id=1, replica_groups=mesh['gx'=8,'gy'=4] {'gx','gy'}, use_global_device_ids=true, to_apply=%region_2.3 | all-reduce | flops 16 | bytes 128 | tf_op jit(solution)/shard_map/psum | solution.py:60
  48.2 1.7 collective-permute-start.3
  50.3 6.7 %collective-permute-done.2 = f32[3,1,64,4,128]{4,3,2,1,0:T(4,128)S(1)} collective-permute-done((f32[3,1,64,4,128]{4,3,2,1,0:T(4,128)S(1)}, f32[3,1,64,4,128]{4,3,2,1,0:T(4,128)S(1)}, u32[]{:S(2)}, u32[]{:S(2)}) %collective-permute-start.2) | collective-permute-done | bytes 393248 | tf_op jit(solution)/shard_map/ppermute | solution.py:19
  57.0 2.5 collective-permute-done.3
  60.6 285.0 %while.10 = (s32[]{:T(128)}, f32[32,3,128]{2,0,1:T(8,128)}, s32[32]{0:T(128)S(1)}, s32[]{:T(128)}, s32[32,16]{1,0:T(8,128)S(1)}, /*index=5*/f32[576,4,128]{2,1,0...) while((s32[]{:T(128)}, f32[32,3,128]{2,0,1:T(8,128)}, ...), condition=%wide.region_8.9_spmd, body=%wide.region_3.8_spmd.sunk | while | flops 5021112 | bytes 4401582 | solution.py:81
  68.2 1.3 dynamic_update_slice.5
  77.1 1.3 dynamic_update_slice.5
  86.0 1.3 dynamic_update_slice.5
  94.9 1.3 dynamic_update_slice.5
  103.8 1.3 dynamic_update_slice.5
  112.7 1.3 dynamic_update_slice.5
  121.6 1.3 dynamic_update_slice.5
  130.5 1.3 dynamic_update_slice.5
  139.4 1.3 dynamic_update_slice.5
  148.3 1.3 dynamic_update_slice.5
  157.2 1.3 dynamic_update_slice.5
  166.1 1.3 dynamic_update_slice.5
  175.1 1.3 dynamic_update_slice.5
  184.0 1.3 dynamic_update_slice.5
  192.9 1.3 dynamic_update_slice.5
  210.7 1.3 dynamic_update_slice.5
  281.9 1.3 dynamic_update_slice.5
  290.8 1.3 dynamic_update_slice.5
  299.7 1.3 dynamic_update_slice.5
  308.6 1.3 dynamic_update_slice.5
  317.6 1.3 dynamic_update_slice.5
  326.5 1.3 dynamic_update_slice.5
  335.4 1.3 dynamic_update_slice.5
  344.3 1.3 dynamic_update_slice.5
  (543 shorter events, 126.2 us)
Async XLA Ops:
  0.0 47.2 %collective-permute-start = (f32[1,1,64,4,128]{4,3,2,1,0:T(4,128)}, f32[1,1,64,4,128]{4,3,2,1,0:T(4,128)S(1)}, u32[]{:S(2)}, u32[]{:S(2)}) collective-permute-start(f32[1,1,64,4,128]{4,3,2,1,0:T(4,128)} %param.6), channel_id=1, source_target_pairs={{0,4},{4,8},{8,12},{12,16},{16,20},{20,24},{24,28},{28,0},{1,5},{5... | collective-permute-start | bytes 393224 | tf_op jit(solution)/shard_map/ppermute | solution.py:19
  2.9 45.2 %collective-permute-start.1 = (f32[1,1,64,4,128]{4,3,2,1,0:T(4,128)}, f32[1,1,64,4,128]{4,3,2,1,0:T(4,128)S(1)}, u32[]{:S(2)}, u32[]{:S(2)}) collective-permute-start(f32[1,1,64,4,128]{4,3,2,1,0:T(4,128)} %param.6), channel_id=1, source_target_pairs={{4,0},{8,4},{12,8},{16,12},{20,16},{24,20},{28,24},{0,28},{5,1},{9... | collective-permute-start | bytes 393224 | tf_op jit(solution)/shard_map/ppermute | solution.py:22
  48.2 8.8 %collective-permute-start.2 = (f32[3,1,64,4,128]{4,3,2,1,0:T(4,128)S(1)}, f32[3,1,64,4,128]{4,3,2,1,0:T(4,128)S(1)}, u32[]{:S(2)}, u32[]{:S(2)}) collective-permute-start(f32[3,1,64,4,128]{4,3,2,1,0:T(4,128)S(1)} %constant_dynamic-update-slice_fusion), channel_id=1, source_target_pairs={{0,1},{1,2},{2,3},{3,0},{4,5},{5,6},{6,7},{7,4},{8,9},{9,10},{10,1... | collective-permute-start | bytes 1179656 | tf_op jit(solution)/shard_map/ppermute | solution.py:19
  48.2 11.2 %collective-permute-start.3 = (f32[3,1,64,4,128]{4,3,2,1,0:T(4,128)S(1)}, f32[3,1,64,4,128]{4,3,2,1,0:T(4,128)S(1)}, u32[]{:S(2)}, u32[]{:S(2)}) collective-permute-start(f32[3,1,64,4,128]{4,3,2,1,0:T(4,128)S(1)} %constant_dynamic-update-slice_fusion), channel_id=1, source_target_pairs={{1,0},{2,1},{3,2},{0,3},{5,4},{6,5},{7,6},{4,7},{9,8},{10,9},{11,1... | collective-permute-start | bytes 1179656 | tf_op jit(solution)/shard_map/ppermute | solution.py:22
where the time goes:
time: 350 us; the launch traced here: 346 us
  loops' own time  131 us (37%)
  local copies, waits for them, and re-layouts  104 us (30%)
  other arithmetic  55.3 us (16%)
  blocking collectives  38.1 us (11%)
  waiting for transfers between devices  9.19 us (3%)
  starting transfers between devices  7.77 us (2%)
    another operation x1, loops' own time, body(): result = lax.map(one_slot, jnp.arange(slots, dtype=jnp.int32))  131 us
    dynamic_update_slice x64, local copies, waits for them, and re-layouts, body(): result = lax.map(one_slot, jnp.arange(slots, dtype=jnp.int32))  42.7 us
    psum x1, blocking collectives, body(): cell_mass = lax.psum(partial_mass, ('gx', 'gy'))  38.1 us
    dynamic_slice x32, local copies, waits for them, and re-layouts, one_slot(): target = local[slot_index]  22 us
    gather x32, local copies, waits for them, and re-layouts, one_slot(): near = pair_accel(target, table[lists[slot_index]])  18.8 us
    dynamic_slice x32, local copies, waits for them, and re-layouts, body(): result = lax.map(one_slot, jnp.arange(slots, dtype=jnp.int32))  18.4 us
    reduce_sum x32, other arithmetic, pair_accel(): return jnp.sum(weight[:, None, :, :] * offset, axis=(0, 3))  15.1 us
    mul x32, other arithmetic, pair_accel(): weight = sources[:, 3, None, :] * dist_sq ** (-1.5)  13.2 us
  transfers between devices with their start and end apart: 4, of which 2 were waited for; matrix products, arithmetic and copies ran while one was open for 1% of the time, Pallas kernels for 0%

commit v1 on v0

v1 whole, which is shorter than its diff:
```python
import functools

import jax
import jax.numpy as jnp
from jax import lax
from jax.experimental import pallas as pl
from jax.experimental.pallas import tpu as pltpu
from jax.sharding import PartitionSpec as P

SUBC = 2
F32 = jnp.float32
BF16 = jnp.bfloat16

soft_near = 0.05
soft_far = 1.0
middle = 0.5


def swap(block, axis, odd):
    count = lax.axis_size(axis)
    pairs = []
    for low in range(odd, count, 2):
        high = (low + 1) % count
        pairs += [(low, high), (high, low)]
    return lax.ppermute(block, axis, pairs)


def total_over(values, axes):
    for axis in axes:
        count = lax.axis_size(axis)
        if count & (count - 1):
            values = lax.psum(values, axis)
            continue
        step = 1
        while step < count:
            values = values + lax.ppermute(values, axis, [(i, i ^ step) for i in range(count)])
            step *= 2
    return values


def split3(v):
    high = v.astype(BF16).astype(F32)
    rest = v - high
    mid = rest.astype(BF16).astype(F32)
    return high, mid, rest - mid


def source_rows(x, y, z):
    rows = []
    for v in (x, y, z):
        high, mid, low = split3(-2.0 * v)
        rows += [high, high, high, mid, mid, low]
    return rows + list(split3((x * x + y * y) + z * z))


def target_rows(x, y, z):
    rows = []
    for v in (x, y, z):
        high, mid, low = split3(v)
        rows += [high, mid, low, high, mid, high]
    one = jnp.ones_like(x)
    rows += [one, one, one]
    rows += list(split3(((x * x + y * y) + z * z) + soft_near * soft_near))
    return rows


def forces(place, limit, lists, cell_mass, *refs, count_blocks, half_gy):
    pieces, out = refs[:9], refs[9]
    table, picked, feature, moment, sems = refs[10:]
    slots, entries = lists.shape
    total = cell_mass.shape[0]
    rows = count_blocks * 4
    depth = feature.shape[1]
    even_x, even_y = place[2], place[3]

    copies = []
    for p in range(9):
        row, col = p // 3, p % 3
        a = (1, 2 * even_x, 2 - 2 * even_x)[row]
        b = (1, 2 * even_y, 2 - 2 * even_y)[col]
        at = pl.multiple_of((3 * a + b) * rows, rows)
        copy = pltpu.make_async_copy(pieces[p], table.at[pl.ds(at, rows), :], sems.at[p])
        copy.start()
        copies.append(copy)
    feature[:, 21:24, :] = jnp.ones_like(feature[:, 21:24, :])
    feature[:, 24:depth, :] = jnp.zeros_like(feature[:, 24:depth, :])
    moment[...] = jnp.zeros_like(moment)
    for copy in copies:
        copy.wait()

    line = lax.broadcasted_iota(jnp.int32, (rows, table.shape[1]), 0) % 4
    for a in range(3):
        for b in range(3):
            if (a, b) != (1, 1):
                at = (3 * a + b) * rows
                moved = jnp.where(line == 0, float(a - 1), jnp.where(line == 1, float(b - 1), 0.0))
                table[at : at + rows, :] = table[at : at + rows, :] + moved

    home = 4 * rows

    def one_slot(slot, carry):
        for k in range(entries):
            at = pl.multiple_of(lists[slot, k] * 4, 4)
            picked[4 * k : 4 * k + 4, :] = table[pl.ds(at, 4), :]
        x, y, z, mass = [picked[pl.ds(c, entries, stride=4), :] for c in range(4)]
        x, y, z = x - middle, y - middle, z - middle
        for i, row in enumerate(source_rows(x, y, z)):
            feature[:, i, :] = row
        for c, value in enumerate((mass * x, mass * y, mass * z, mass)):
            for p, part in enumerate(split3(value)):
                moment[:, 4 * p + c, :] = part
        target = table[pl.ds(pl.multiple_of(home + slot * 4, 4), 4), :]
        tx, ty, tz = [target[c : c + 1] - middle for c in range(3)]
        near = target_rows(tx, ty, tz)
        near += [jnp.zeros_like(tx)] * (depth - len(near))
        near = jnp.concatenate(near, axis=0).astype(BF16)
        sums = jnp.zeros((moment.shape[1], table.shape[1]), F32)
        for k in range(0, entries, 2):
            here = jnp.concatenate([feature[k], feature[k + 1]], axis=1).astype(BF16)
            dist_sq = lax.dot_general(here, near, (((0,), (0,)), ((), ())), preferred_element_type=F32)
            inverse = lax.rsqrt(dist_sq)
            weight = inverse * inverse * inverse
            parts = jnp.concatenate([moment[k], moment[k + 1]], axis=1).astype(BF16)
            high = weight.astype(BF16)
            low = (weight - high.astype(F32)).astype(BF16)
            sums += jnp.dot(parts, high, preferred_element_type=F32)
            sums += jnp.dot(parts, low, preferred_element_type=F32)
        sums = (sums[0:4] + sums[4:8]) + sums[8:12]
        for c, t in enumerate((tx, ty, tz)):
            out[slot, c : c + 1, :] = sums[c : c + 1] - t * sums[3:4]
        return carry

    lax.fori_loop(0, limit[0], one_slot, 0)

    corner = (place[0].astype(F32), place[1].astype(F32), 0.0)
    position = [table[pl.ds(home + c, slots, stride=4), :] + corner[c] for c in range(3)]

    def one_cell(cell, carry):
        group, sub_cell = cell // SUBC, cell % SUBC
        centre = (
            (2 * (group // half_gy) + 1).astype(F32),
            (2 * (group % half_gy) + 1).astype(F32),
            (sub_cell.astype(F32) + 0.5) * (1.0 / SUBC),
        )
        offset = [centre[c] - position[c] for c in range(3)]
        dist_sq = (offset[0] * offset[0] + offset[1] * offset[1]) + offset[2] * offset[2]
        inverse = lax.rsqrt(dist_sq + soft_far * soft_far)
        weight = cell_mass[cell] * (inverse * inverse * inverse)
        return tuple(carry[c] + weight * offset[c] for c in range(3))

    far = lax.fori_loop(0, total, one_cell, tuple(jnp.zeros_like(v) for v in position))
    active = lax.broadcasted_iota(jnp.int32, far[0].shape, 0) < limit[0]
    for c in range(3):
        out[:, c, :] = jnp.where(active, out[:, c, :] + far[c], 0.0)


def body(blocks, active_counts, pair_lists, cell_ids):
    count_blocks, width = blocks.shape[2], blocks.shape[4]
    slots, entries = pair_lists.shape[2:]
    half_gy = lax.axis_size("gy") // 2
    total = lax.axis_size("gx") // 2 * half_gy * SUBC
    own = blocks.reshape(count_blocks * 4, width)

    first_x = swap(own, "gx", 0)
    first_y = swap(own, "gy", 0)
    second_y = swap(own, "gy", 1)
    second_x = swap(own, "gx", 1)
    pieces = [own, first_y, second_y]
    for row in (first_x, second_x):
        pieces += [row, swap(row, "gy", 0), swap(row, "gy", 1)]

    block_mass = jnp.sum(blocks[0, 0, :, 3, :], axis=-1)
    member = cell_ids[0, 0][:, None] == jnp.arange(total, dtype=jnp.int32)[None, :]
    partial_mass = jnp.sum(jnp.where(member, block_mass[:, None], 0.0), axis=0)
    cell_mass = total_over(partial_mass, ("gx", "gy"))

    row, col = lax.axis_index("gx"), lax.axis_index("gy")
    place = jnp.stack([row, col, 1 - row % 2, 1 - col % 2]).astype(jnp.int32)
    smem = pl.BlockSpec(memory_space=pltpu.SMEM)
    result = pl.pallas_call(
        functools.partial(forces, count_blocks=count_blocks, half_gy=half_gy),
        out_shape=jax.ShapeDtypeStruct((slots, 3, width), F32),
        in_specs=[smem] * 4 + [pl.BlockSpec(memory_space=pl.ANY)] * 9,
        out_specs=pl.BlockSpec(memory_space=pltpu.VMEM),
        scratch_shapes=[
            pltpu.VMEM((9 * count_blocks * 4, width), F32),
            pltpu.VMEM((entries * 4, width), F32),
            pltpu.VMEM((entries, 32, width), F32),
            pltpu.VMEM((entries, 16, width), F32),
            pltpu.SemaphoreType.DMA((9,)),
        ],
        compiler_params=pltpu.CompilerParams(vmem_limit_bytes=16 * 2**20),
    )(place, active_counts.reshape(1), pair_lists[0, 0], cell_mass, *pieces)
    return result[None, None]


def solution(mesh):
    in_specs = (
        P("gx", "gy", None, None, None),
        P("gx", "gy"),
        P("gx", "gy", None, None),
        P("gx", "gy", None),
    )
    out_specs = P("gx", "gy", None, None, None)
    return jax.shard_map(body, mesh=mesh, in_specs=in_specs, out_specs=out_specs, check_vma=False)
```

time: 350 us -> 56.7 us (0.16); the launches traced: 346 us -> 57.2 us
  loops' own time: 131 us -> 0 us
  local copies, waits for them, and re-layouts: 104 us -> 1.4 us
  other arithmetic: 55.3 us -> 2.35 us
  blocking collectives: 38.1 us -> 0 us
  Pallas kernels: 0 us -> 24.8 us
  waiting for transfers between devices: 9.19 us -> 15.1 us
  starting transfers between devices: 7.77 us -> 12.9 us
    another operation x1 -> x0, loops' own time: 131 us -> none  [body(): result = lax.map(one_slot, jnp.arange(slots, dtype=jnp.int32))]
    dynamic_update_slice x64 -> x0, local copies, waits for them, and re-layouts: 42.7 us -> none  [body(): result = lax.map(one_slot, jnp.arange(slots, dtype=jnp.int32))]
    dynamic_slice x64 -> x0, local copies, waits for them, and re-layouts: 40.4 us -> none  [the longest x32 22 us: one_slot(): target = local[slot_index]]
    psum x1 -> x0, blocking collectives: 38.1 us -> none  [body(): cell_mass = lax.psum(partial_mass, ('gx', 'gy'))]
    reduce_sum x129 -> x1, other arithmetic: 34.7 us -> 1.49 us  [body(): block_mass = jnp.sum(blocks[0, 0, :, 3, :], axis=-1)]
    pallas_call x0 -> x1, Pallas kernels: none -> 24.8 us  [body(): pl.pallas_call(functools.partial(forces, count_blocks=count_blocks, half_...]
    gather x32 -> x0, local copies, waits for them, and re-layouts: 18.8 us -> none  [one_slot(): near = pair_accel(target, table[lists[slot_index]])]
    mul x64 -> x0, other arithmetic: 15.6 us -> none  [the longest x32 13.2 us: pair_accel(): weight = sources[:, 3, None, :] * dist_sq ** (-1.5)]
  transfers between devices with their start and end apart: 4 -> 13, of which waited for: 2 -> 7; matrix products, arithmetic and copies ran while one was open for 1% -> 5% of each run, Pallas kernels for 0% -> 0%
where the time goes in v1:
time: 56.7 us; the launch traced here: 57.2 us
  Pallas kernels  24.8 us (44%)
  waiting for transfers between devices  15.1 us (27%)
  starting transfers between devices  12.9 us (23%)
  other arithmetic  2.35 us (4%)
  local copies, waits for them, and re-layouts  1.4 us (2%)
  between operations  0.68 us (1%)
    pallas_call x1, Pallas kernels, body(): pl.pallas_call(functools.partial(forces, count_blocks=count_blocks, half_...  24.8 us
    ppermute x5, waiting for transfers between devices, total_over(): lax.ppermute(values, axis, [(i, i ^ step) for i in range(count)])  11.7 us
    ppermute x8, starting transfers between devices, swap(): return lax.ppermute(block, axis, pairs)  8.86 us
    ppermute x5, starting transfers between devices, total_over(): lax.ppermute(values, axis, [(i, i ^ step) for i in range(count)])  4.05 us
    ppermute x8, waiting for transfers between devices, swap(): return lax.ppermute(block, axis, pairs)  3.33 us
    reduce_sum x1, other arithmetic, body(): block_mass = jnp.sum(blocks[0, 0, :, 3, :], axis=-1)  1.49 us
  transfers between devices with their start and end apart: 13, of which 7 were waited for; matrix products, arithmetic and copies ran while one was open for 5% of the time, Pallas kernels for 0%

profile of v1, /device:TPU:0, one launch (start us, length us, event | category | flops | bytes accessed | tf_op | source)
XLA Modules:
  0.0 57.2 jit_solution(8054734974271573704)
XLA Ops:
  0.0 6.0 %collective-permute-start.10 = (f32[256,128]{1,0:T(8,128)}, f32[256,128]{1,0:T(8,128)S(1)}, u32[]{:S(2)}, u32[]{:S(2)}) collective-permute-start(f32[256,128]{1,0:T(8,128)} %bitcast.11), channel_id=1, source_target_pairs={{4,8},{8,4},{12,16},{16,12},{20,24},{24,20},{28,0},{0,28},{5,9},{9... | collective-permute-start | bytes 393224 | tf_op jit(solution)/shard_map/ppermute | solution.py:25
  6.0 0.0 collective-permute-start.7
  6.0 0.7 %collective-permute-start.6 = (f32[256,128]{1,0:T(8,128)}, f32[256,128]{1,0:T(8,128)S(1)}, u32[]{:S(2)}, u32[]{:S(2)}) collective-permute-start(f32[256,128]{1,0:T(8,128)} %bitcast.13), channel_id=1, source_target_pairs={{1,2},{2,1},{3,0},{0,3},{5,6},{6,5},{7,4},{4,7},{9,10},{10,9},{11,... | collective-permute-start | bytes 393224 | tf_op jit(solution)/shard_map/ppermute | solution.py:25
  6.7 1.5 %slice_reduce_fusion = f32[64]{0:T(128)S(1)} fusion(f32[1,1,64,4,128]{4,3,2,1,0:T(4,128)} %param.4), kind=kLoop, calls=%fused_computation | loop fusion | flops 8128 | bytes 33024 | tf_op jit(solution)/shard_map/reduce_sum | solution.py:172
  8.2 0.8 %select_reduce_fusion = f32[16]{0:T(128)S(1)} fusion(f32[64]{0:T(128)S(1)} %slice_reduce_fusion, s32[64]{0:T(128)} %bitcast.17), kind=kLoop, calls=%fused_computation.1 | loop fusion | flops 3056 | bytes 576 | tf_op jit(solution)/shard_map/reduce_sum | solution.py:174
  8.9 1.8 %collective-permute-start = (f32[16]{0:T(128)S(1)}, f32[16]{0:T(128)S(1)}, u32[]{:S(2)}, u32[]{:S(2)}) collective-permute-start(f32[16]{0:T(128)S(1)} %select_reduce_fusion), channel_id=1, source_target_pairs={{0,4},{4,0},{8,12},{12,8},{16,20},{20,16},{24,28},{28,24},{1,5},{5... | collective-permute-start | bytes 200 | tf_op jit(solution)/shard_map/ppermute | solution.py:36
  10.7 1.9 %collective-permute-done = f32[16]{0:T(128)S(1)} collective-permute-done((f32[16]{0:T(128)S(1)}, f32[16]{0:T(128)S(1)}, u32[]{:S(2)}, u32[]{:S(2)}) %collective-permute-start) | collective-permute-done | bytes 96 | tf_op jit(solution)/shard_map/ppermute | solution.py:36
  12.6 0.0 collective-permute-start.1
  12.6 3.5 %collective-permute-done.1 = f32[16]{0:T(128)S(1)} collective-permute-done((f32[16]{0:T(128)S(1)}, f32[16]{0:T(128)S(1)}, u32[]{:S(2)}, u32[]{:S(2)}) %collective-permute-start.1) | collective-permute-done | bytes 96 | tf_op jit(solution)/shard_map/ppermute | solution.py:36
  16.2 0.7 %collective-permute-start.2 = (f32[16]{0:T(128)S(1)}, f32[16]{0:T(128)S(1)}, u32[]{:S(2)}, u32[]{:S(2)}) collective-permute-start(f32[16]{0:T(128)S(1)} %add.25), channel_id=1, source_target_pairs={{0,16},{4,20},{8,24},{12,28},{16,0},{20,4},{24,8},{28,12},{1,17},{... | collective-permute-start | bytes 200 | tf_op jit(solution)/shard_map/ppermute | solution.py:36
  16.9 3.7 %collective-permute-done.2 = f32[16]{0:T(128)S(1)} collective-permute-done((f32[16]{0:T(128)S(1)}, f32[16]{0:T(128)S(1)}, u32[]{:S(2)}, u32[]{:S(2)}) %collective-permute-start.2) | collective-permute-done | bytes 96 | tf_op jit(solution)/shard_map/ppermute | solution.py:36
  20.6 0.0 collective-permute-start.3
  20.6 0.5 collective-permute-start.5
  21.1 0.6 %collective-permute-done.3 = f32[16]{0:T(128)S(1)} collective-permute-done((f32[16]{0:T(128)S(1)}, f32[16]{0:T(128)S(1)}, u32[]{:S(2)}, u32[]{:S(2)}) %collective-permute-start.3) | collective-permute-done | bytes 96 | tf_op jit(solution)/shard_map/ppermute | solution.py:36
  21.7 1.5 %collective-permute-start.4 = (f32[16]{0:T(128)S(1)}, f32[16]{0:T(128)S(1)}, u32[]{:S(2)}, u32[]{:S(2)}) collective-permute-start(f32[16]{0:T(128)S(1)} %add.27), channel_id=1, source_target_pairs={{0,2},{1,3},{2,0},{3,1},{4,6},{5,7},{6,4},{7,5},{8,10},{9,11},{10,... | collective-permute-start | bytes 200 | tf_op jit(solution)/shard_map/ppermute | solution.py:36
  23.3 0.0 collective-permute-done.10.refs_6_
  23.3 0.0 collective-permute-start.12
  23.3 2.0 %collective-permute-done.4 = f32[16]{0:T(128)S(1)} collective-permute-done((f32[16]{0:T(128)S(1)}, f32[16]{0:T(128)S(1)}, u32[]{:S(2)}, u32[]{:S(2)}) %collective-permute-start.4) | collective-permute-done | bytes 96 | tf_op jit(solution)/shard_map/ppermute | solution.py:36
  25.3 0.0 collective-permute-start.11
  25.3 0.0 collective-permute-done.7.refs_3_
  25.3 1.6 %collective-permute-start.9 = (f32[256,128]{1,0:T(8,128)S(1)}, f32[256,128]{1,0:T(8,128)S(1)}, u32[]{:S(2)}, u32[]{:S(2)}) collective-permute-start(f32[256,128]{1,0:T(8,128)S(1)} %collective-permute-done.7.refs_3_), channel_id=1, source_target_pairs={{1,2},{2,1},{3,0},{0,3},{5,6},{6,5},{7,4},{4,7},{9,10},{10,9},{11,... | collective-permute-start | bytes 393224 | tf_op jit(solution)/shard_map/ppermute | solution.py:25
  26.9 0.0 collective-permute-done.6.refs_2_
  26.9 0.0 collective-permute-start.8
  27.6 0.8 %copy.7 = s32[1,1,32,16]{3,2,1,0:T(8,128)S(1)} copy(s32[1,1,32,16]{2,3,1,0:T(8,128)} %param.6) | data formatting | bytes 4096 | tf_op args[2]
  28.4 0.1 pad_add_fusion.place
  28.4 0.0 collective-permute-done.5.refs_1_
  28.4 0.5 collective-permute-done.12.refs_8_
  29.0 0.0 collective-permute-done.11.refs_7_
  29.0 2.8 %collective-permute-done.9.refs_5_ = f32[256,128]{1,0:T(8,128)S(1)} collective-permute-done((f32[256,128]{1,0:T(8,128)S(1)}, f32[256,128]{1,0:T(8,128)S(1)}, u32[]{:S(2)}, u32[]{:S(2)}) %collective-permute-start.9) | collective-permute-done | bytes 131104 | tf_op jit(solution)/shard_map/ppermute | solution.py:25
  31.8 0.0 collective-permute-done.8.refs_4_
  31.8 24.8 %shard_map.46 = f32[32,3,128]{2,1,0:T(4,128)S(1)} custom-call(s32[4]{0:T(128)S(1)} %pad_add_fusion.place, s32[1]{0:T(128)} %bitcast.9.limit, s32[32,16]{1,0:T(8,128)S(1)} %bitcast.16, f32[16]{0:T(128)S(1)} %add.28.cell_mass, f32[256,128]{1,0:T(8,128)S(1)} %bitcast.15, f32[256,128]{1,0:T(8,128)S(1)} %collective-permute-done.5.refs_1_, ...), custom_call_target="tpu_custom_call" | custom-call | tf_op jit(solution)/shard_map/pallas_call | solution.py:180
  56.5 0.6 %copy.8 = f32[1,1,32,3,128]{4,2,3,1,0:T(8,128)} copy(f32[1,1,32,3,128]{4,3,2,1,0:T(4,128)S(1)} %bitcast.10) | data formatting | bytes 98304 | tf_op jit(solution)/shard_map/broadcast_in_dim | solution.py:194
  (7 shorter events, 0.0 us)
Async XLA Ops:
  0.0 31.8 %copy-start = (f32[1,1,64,4,128]{4,3,2,1,0:T(4,128)S(1)}, f32[1,1,64,4,128]{4,3,2,1,0:T(4,128)}, u32[]{:S(2)}) copy-start(f32[1,1,64,4,128]{4,3,2,1,0:T(4,128)} %param.4) | copy-start | bytes 393220
  0.0 23.3 %collective-permute-start.10 = (f32[256,128]{1,0:T(8,128)}, f32[256,128]{1,0:T(8,128)S(1)}, u32[]{:S(2)}, u32[]{:S(2)}) collective-permute-start(f32[256,128]{1,0:T(8,128)} %bitcast.11), channel_id=1, source_target_pairs={{4,8},{8,4},{12,16},{16,12},{20,24},{24,20},{28,0},{0,28},{5,9},{9... | collective-permute-start | bytes 393224 | tf_op jit(solution)/shard_map/ppermute | solution.py:25
  6.0 19.3 %collective-permute-start.7 = (f32[256,128]{1,0:T(8,128)}, f32[256,128]{1,0:T(8,128)S(1)}, u32[]{:S(2)}, u32[]{:S(2)}) collective-permute-start(f32[256,128]{1,0:T(8,128)} %bitcast.12), channel_id=1, source_target_pairs={{0,4},{4,0},{8,12},{12,8},{16,20},{20,16},{24,28},{28,24},{1,5},{5... | collective-permute-start | bytes 393224 | tf_op jit(solution)/shard_map/ppermute | solution.py:25
  6.0 20.9 %collective-permute-start.6 = (f32[256,128]{1,0:T(8,128)}, f32[256,128]{1,0:T(8,128)S(1)}, u32[]{:S(2)}, u32[]{:S(2)}) collective-permute-start(f32[256,128]{1,0:T(8,128)} %bitcast.13), channel_id=1, source_target_pairs={{1,2},{2,1},{3,0},{0,3},{5,6},{6,5},{7,4},{4,7},{9,10},{10,9},{11,... | collective-permute-start | bytes 393224 | tf_op jit(solution)/shard_map/ppermute | solution.py:25
  8.9 3.7 %collective-permute-start = (f32[16]{0:T(128)S(1)}, f32[16]{0:T(128)S(1)}, u32[]{:S(2)}, u32[]{:S(2)}) collective-permute-start(f32[16]{0:T(128)S(1)} %select_reduce_fusion), channel_id=1, source_target_pairs={{0,4},{4,0},{8,12},{12,8},{16,20},{20,16},{24,28},{28,24},{1,5},{5... | collective-permute-start | bytes 200 | tf_op jit(solution)/shard_map/ppermute | solution.py:36
  12.6 3.5 %collective-permute-start.1 = (f32[16]{0:T(128)S(1)}, f32[16]{0:T(128)S(1)}, u32[]{:S(2)}, u32[]{:S(2)}) collective-permute-start(f32[16]{0:T(128)S(1)} %add.24), channel_id=1, source_target_pairs={{0,8},{4,12},{8,0},{12,4},{16,24},{20,28},{24,16},{28,20},{1,9},{5... | collective-permute-start | bytes 200 | tf_op jit(solution)/shard_map/ppermute | solution.py:36
  16.2 4.4 %collective-permute-start.2 = (f32[16]{0:T(128)S(1)}, f32[16]{0:T(128)S(1)}, u32[]{:S(2)}, u32[]{:S(2)}) collective-permute-start(f32[16]{0:T(128)S(1)} %add.25), channel_id=1, source_target_pairs={{0,16},{4,20},{8,24},{12,28},{16,0},{20,4},{24,8},{28,12},{1,17},{... | collective-permute-start | bytes 200 | tf_op jit(solution)/shard_map/ppermute | solution.py:36
  20.6 1.1 %collective-permute-start.3 = (f32[16]{0:T(128)S(1)}, f32[16]{0:T(128)S(1)}, u32[]{:S(2)}, u32[]{:S(2)}) collective-permute-start(f32[16]{0:T(128)S(1)} %add.26), channel_id=1, source_target_pairs={{0,1},{1,0},{2,3},{3,2},{4,5},{5,4},{6,7},{7,6},{8,9},{9,8},{10,11... | collective-permute-start | bytes 200 | tf_op jit(solution)/shard_map/ppermute | solution.py:36
  20.6 7.8 %collective-permute-start.5 = (f32[256,128]{1,0:T(8,128)}, f32[256,128]{1,0:T(8,128)S(1)}, u32[]{:S(2)}, u32[]{:S(2)}) collective-permute-start(f32[256,128]{1,0:T(8,128)} %bitcast.14), channel_id=1, source_target_pairs={{0,1},{1,0},{2,3},{3,2},{4,5},{5,4},{6,7},{7,6},{8,9},{9,8},{10,11... | collective-permute-start | bytes 393224 | tf_op jit(solution)/shard_map/ppermute | solution.py:25
  21.7 3.5 %collective-permute-start.4 = (f32[16]{0:T(128)S(1)}, f32[16]{0:T(128)S(1)}, u32[]{:S(2)}, u32[]{:S(2)}) collective-permute-start(f32[16]{0:T(128)S(1)} %add.27), channel_id=1, source_target_pairs={{0,2},{1,3},{2,0},{3,1},{4,6},{5,7},{6,4},{7,5},{8,10},{9,11},{10,... | collective-permute-start | bytes 200 | tf_op jit(solution)/shard_map/ppermute | solution.py:36
  23.3 5.7 %collective-permute-start.12 = (f32[256,128]{1,0:T(8,128)S(1)}, f32[256,128]{1,0:T(8,128)S(1)}, u32[]{:S(2)}, u32[]{:S(2)}) collective-permute-start(f32[256,128]{1,0:T(8,128)S(1)} %collective-permute-done.10.refs_6_), channel_id=1, source_target_pairs={{1,2},{2,1},{3,0},{0,3},{5,6},{6,5},{7,4},{4,7},{9,10},{10,9},{11,... | collective-permute-start | bytes 393224 | tf_op jit(solution)/shard_map/ppermute | solution.py:25
  25.3 3.7 %collective-permute-start.11 = (f32[256,128]{1,0:T(8,128)S(1)}, f32[256,128]{1,0:T(8,128)S(1)}, u32[]{:S(2)}, u32[]{:S(2)}) collective-permute-start(f32[256,128]{1,0:T(8,128)S(1)} %collective-permute-done.10.refs_6_), channel_id=1, source_target_pairs={{0,1},{1,0},{2,3},{3,2},{4,5},{5,4},{6,7},{7,6},{8,9},{9,8},{10,11... | collective-permute-start | bytes 393224 | tf_op jit(solution)/shard_map/ppermute | solution.py:25
  25.3 6.5 %collective-permute-start.9 = (f32[256,128]{1,0:T(8,128)S(1)}, f32[256,128]{1,0:T(8,128)S(1)}, u32[]{:S(2)}, u32[]{:S(2)}) collective-permute-start(f32[256,128]{1,0:T(8,128)S(1)} %collective-permute-done.7.refs_3_), channel_id=1, source_target_pairs={{1,2},{2,1},{3,0},{0,3},{5,6},{6,5},{7,4},{4,7},{9,10},{10,9},{11,... | collective-permute-start | bytes 393224 | tf_op jit(solution)/shard_map/ppermute | solution.py:25
  26.9 4.8 %collective-permute-start.8 = (f32[256,128]{1,0:T(8,128)S(1)}, f32[256,128]{1,0:T(8,128)S(1)}, u32[]{:S(2)}, u32[]{:S(2)}) collective-permute-start(f32[256,128]{1,0:T(8,128)S(1)} %collective-permute-done.7.refs_3_), channel_id=1, source_target_pairs={{0,1},{1,0},{2,3},{3,2},{4,5},{5,4},{6,7},{7,6},{8,9},{9,8},{10,11... | collective-permute-start | bytes 393224 | tf_op jit(solution)/shard_map/ppermute | solution.py:25

commit v2 on v1

v2 whole, which is shorter than its diff:
```python
import functools
import math

import jax
import jax.numpy as jnp
from jax import lax
from jax.experimental import pallas as pl
from jax.experimental.pallas import tpu as pltpu
from jax.sharding import PartitionSpec as P

SUBC = 2
F32 = jnp.float32
BF16 = jnp.bfloat16

soft_near = 0.05
soft_far = 1.0
middle = 0.5


def swap(block, axis, odd):
    count = lax.axis_size(axis)
    pairs = []
    for low in range(odd, count, 2):
        high = (low + 1) % count
        pairs += [(low, high), (high, low)]
    return lax.ppermute(block, axis, pairs)


def total_over(values, axes):
    for axis in axes:
        count = lax.axis_size(axis)
        if count & (count - 1):
            values = lax.psum(values, axis)
            continue
        step = 1
        while step < count:
            values = values + lax.ppermute(values, axis, [(i, i ^ step) for i in range(count)])
            step *= 2
    return values


def split3(v):
    high = v.astype(BF16).astype(F32)
    rest = v - high
    mid = rest.astype(BF16).astype(F32)
    return high, mid, rest - mid


def roll(v, step):
    return pltpu.roll(v, step, 0)


def halves(low_half, pairs):
    upper = [jnp.where(low_half, first, roll(second, 4)) for first, second in pairs]
    lower = [jnp.where(low_half, roll(first, 4), second) for first, second in pairs]
    return [jnp.concatenate(rows, axis=0).astype(BF16) for rows in (upper, lower)]


def square_norm(is_mass, centred):
    square = jnp.where(is_mass, 0.0, centred)
    square = square * square
    return (roll(square, 1) + roll(square, 2)) + roll(square, 3)


def source_tile(tile, moved, is_mass, low_half):
    zero = jnp.zeros_like(tile)
    centred = (tile + moved) - jnp.where(is_mass, 0.0, middle)
    rows = jnp.where(is_mass, square_norm(is_mass, centred), -2.0 * centred)
    high, mid, low = split3(rows)
    high_1, mid_1 = jnp.where(is_mass, 1.0, high), jnp.where(is_mass, 1.0, mid)
    features = halves(low_half, [(high, high_1), (high_1, mid), (mid_1, low), (zero, zero)])
    mass = jnp.where(is_mass, tile, 0.0)
    mass = (mass + roll(mass, 7)) + (roll(mass, 6) + roll(mass, 5))
    high, mid, low = split3(jnp.where(is_mass, 1.0, centred) * mass)
    return features, halves(low_half, [(high, mid), (low, zero)])


def target_tile(tile, is_mass, low_half):
    zero = jnp.zeros_like(tile)
    centred = tile - middle
    norm = square_norm(is_mass, centred) + soft_near * soft_near
    high, mid, low = split3(jnp.where(is_mass, norm, centred))
    one_high = jnp.where(is_mass, 1.0, high)
    high_mid = jnp.where(is_mass, high, mid)
    mid_low = jnp.where(is_mass, mid, low)
    low_mid = jnp.where(is_mass, low, mid)
    return halves(low_half, [(one_high, high_mid), (mid_low, one_high), (low_mid, one_high), (zero, zero)])


def forces(place, limit, lists, cell_mass, *refs, count_blocks, half_gy, together):
    pieces, out = refs[:9], refs[9]
    table, feature, moment, target, sems = refs[10:]
    slots, entries = lists.shape
    width = table.shape[1]
    total = cell_mass.shape[0]
    rows = count_blocks * 4
    even_x, even_y = place[2], place[3]

    copies = []
    for p in range(9):
        row, col = p // 3, p % 3
        a = (1, 2 * even_x, 2 - 2 * even_x)[row]
        b = (1, 2 * even_y, 2 - 2 * even_y)[col]
        at = pl.multiple_of((3 * a + b) * rows, rows)
        copy = pltpu.make_async_copy(pieces[p], table.at[pl.ds(at, rows), :], sems.at[p])
        copy.start()
        copies.append(copy)
    for copy in copies:
        copy.wait()

    line = lax.broadcasted_iota(jnp.int32, (8, width), 0)
    is_mass, low_half = line % 4 == 3, line < 4
    is_x, is_y = line % 4 == 0, line % 4 == 1
    tiles = count_blocks // 2

    def one_domain(domain, carry):
        step_a = (domain // 3 - 1).astype(F32)
        step_b = (domain % 3 - 1).astype(F32)
        moved = jnp.where(is_x, step_a, jnp.where(is_y, step_b, 0.0))

        def two_tiles(pair, carry):
            for u in range(2):
                at = domain * tiles + pair * 2 + u
                tile = table[pl.ds(pl.multiple_of(at * 8, 8), 8), :]
                features, moments = source_tile(tile, moved, is_mass, low_half)
                for half in range(2):
                    feature[2 * at + half] = features[half]
                    moment[2 * at + half] = moments[half]
            return carry

        return lax.fori_loop(0, tiles // 2, two_tiles, carry)

    lax.fori_loop(0, 9, one_domain, 0)

    home = 4 * rows

    def one_target(pair, carry):
        tile = table[pl.ds(pl.multiple_of(home + pair * 8, 8), 8), :]
        for half, value in enumerate(target_tile(tile, is_mass, low_half)):
            target[2 * pair + half] = value
        return carry

    lax.fori_loop(0, slots // 2, one_target, 0)

    def some_slots(group, carry):
        for u in range(together):
            slot = group * together + u
            near = target[slot]
            sums = jnp.zeros((moment.shape[1], width), F32)
            for k in range(0, entries, 2):
                one, two = lists[slot, k], lists[slot, k + 1]
                here = jnp.concatenate([feature[one], feature[two]], axis=1)
                parts = jnp.concatenate([moment[one], moment[two]], axis=1)
                dist_sq = lax.dot_general(here, near, (((0,), (0,)), ((), ())), preferred_element_type=F32)
                inverse = lax.rsqrt(dist_sq)
                weight = inverse * inverse * inverse
                high = weight.astype(BF16)
                low = (weight - high.astype(F32)).astype(BF16)
                sums += jnp.dot(parts, high, preferred_element_type=F32)
                sums += jnp.dot(parts, low, preferred_element_type=F32)
            sums = (sums[0:4] + sums[4:8]) + sums[8:12]
            own = table[pl.ds(pl.multiple_of(home + slot * 4, 4), 4), :] - middle
            for c in range(3):
                out[slot, c : c + 1, :] = sums[c : c + 1] - own[c : c + 1] * sums[3:4]
        return carry

    lax.fori_loop(0, (limit[0] + together - 1) // together, some_slots, 0)

    corner = (place[0].astype(F32), place[1].astype(F32), 0.0)
    position = [table[pl.ds(home + c, slots, stride=4), :] + corner[c] for c in range(3)]

    def one_cell(cell, carry):
        group, sub_cell = cell // SUBC, cell % SUBC
        centre = (
            (2 * (group // half_gy) + 1).astype(F32),
            (2 * (group % half_gy) + 1).astype(F32),
            (sub_cell.astype(F32) + 0.5) * (1.0 / SUBC),
        )
        offset = [centre[c] - position[c] for c in range(3)]
        dist_sq = (offset[0] * offset[0] + offset[1] * offset[1]) + offset[2] * offset[2]
        inverse = lax.rsqrt(dist_sq + soft_far * soft_far)
        weight = cell_mass[cell] * (inverse * inverse * inverse)
        return tuple(carry[c] + weight * offset[c] for c in range(3))

    far = lax.fori_loop(0, total, one_cell, tuple(jnp.zeros_like(v) for v in position))
    active = lax.broadcasted_iota(jnp.int32, far[0].shape, 0) < limit[0]
    for c in range(3):
        out[:, c, :] = jnp.where(active, out[:, c, :] + far[c], 0.0)


def body(blocks, active_counts, pair_lists, cell_ids):
    count_blocks, width = blocks.shape[2], blocks.shape[4]
    slots, entries = pair_lists.shape[2:]
    half_gy = lax.axis_size("gy") // 2
    total = lax.axis_size("gx") // 2 * half_gy * SUBC
    own = blocks.reshape(count_blocks * 4, width)

    first_x = swap(own, "gx", 0)
    first_y = swap(own, "gy", 0)
    second_y = swap(own, "gy", 1)
    second_x = swap(own, "gx", 1)
    pieces = [own, first_y, second_y]
    for row in (first_x, second_x):
        pieces += [row, swap(row, "gy", 0), swap(row, "gy", 1)]

    block_mass = jnp.sum(blocks[0, 0, :, 3, :], axis=-1)
    member = cell_ids[0, 0][:, None] == jnp.arange(total, dtype=jnp.int32)[None, :]
    partial_mass = jnp.sum(jnp.where(member, block_mass[:, None], 0.0), axis=0)
    cell_mass = total_over(partial_mass, ("gx", "gy"))

    row, col = lax.axis_index("gx"), lax.axis_index("gy")
    place = jnp.stack([row, col, 1 - row % 2, 1 - col % 2]).astype(jnp.int32)
    smem = pl.BlockSpec(memory_space=pltpu.SMEM)
    result = pl.pallas_call(
        functools.partial(forces, count_blocks=count_blocks, half_gy=half_gy, together=math.gcd(slots, 8)),
        out_shape=jax.ShapeDtypeStruct((slots, 3, width), F32),
        in_specs=[smem] * 4 + [pl.BlockSpec(memory_space=pl.ANY)] * 9,
        out_specs=pl.BlockSpec(memory_space=pltpu.VMEM),
        scratch_shapes=[
            pltpu.VMEM((9 * count_blocks * 4, width), F32),
            pltpu.VMEM((9 * count_blocks, 32, width), BF16),
            pltpu.VMEM((9 * count_blocks, 16, width), BF16),
            pltpu.VMEM((slots, 32, width), BF16),
            pltpu.SemaphoreType.DMA((9,)),
        ],
        compiler_params=pltpu.CompilerParams(vmem_limit_bytes=24 * 2**20),
    )(place, active_counts.reshape(1), pair_lists[0, 0], cell_mass, *pieces)
    return result[None, None]


def solution(mesh):
    in_specs = (
        P("gx", "gy", None, None, None),
        P("gx", "gy"),
        P("gx", "gy", None, None),
        P("gx", "gy", None),
    )
    out_specs = P("gx", "gy", None, None, None)
    return jax.shard_map(body, mesh=mesh, in_specs=in_specs, out_specs=out_specs, check_vma=False)
```

time: 56.7 us -> 49.5 us (0.87); the launches traced: 57.2 us -> 49.3 us
  Pallas kernels: 24.8 us -> 16.9 us
    pallas_call x1, Pallas kernels: 24.8 us -> 16.9 us  [body(): pl.pallas_call(functools.partial(forces, count_blocks=count_blocks, half_...]
  transfers between devices with their start and end apart: 13 -> 13, of which waited for: 7 -> 7; matrix products, arithmetic and copies ran while one was open for 5% -> 6% of each run, Pallas kernels for 0% -> 0%
where the time goes in v2:
time: 49.5 us; the launch traced here: 49.3 us
  Pallas kernels  16.9 us (34%)
  waiting for transfers between devices  15.1 us (31%)
  starting transfers between devices  12.9 us (26%)
  other arithmetic  2.35 us (5%)
  local copies, waits for them, and re-layouts  1.4 us (3%)
  between operations  0.68 us (1%)
    pallas_call x1, Pallas kernels, body(): pl.pallas_call(functools.partial(forces, count_blocks=count_blocks, half_...  16.9 us
    ppermute x5, waiting for transfers between devices, total_over(): lax.ppermute(values, axis, [(i, i ^ step) for i in range(count)])  11.7 us
    ppermute x8, starting transfers between devices, swap(): return lax.ppermute(block, axis, pairs)  8.86 us
    ppermute x5, starting transfers between devices, total_over(): lax.ppermute(values, axis, [(i, i ^ step) for i in range(count)])  4.05 us
    ppermute x8, waiting for transfers between devices, swap(): return lax.ppermute(block, axis, pairs)  3.33 us
    reduce_sum x1, other arithmetic, body(): block_mass = jnp.sum(blocks[0, 0, :, 3, :], axis=-1)  1.49 us
  transfers between devices with their start and end apart: 13, of which 7 were waited for; matrix products, arithmetic and copies ran while one was open for 6% of the time, Pallas kernels for 0%

profile of v2, /device:TPU:0, one launch (start us, length us, event | category | flops | bytes accessed | tf_op | source)
XLA Modules:
  0.0 49.3 jit_solution(13431947717951342876)
XLA Ops:
  0.0 6.0 %collective-permute-start.10 = (f32[256,128]{1,0:T(8,128)}, f32[256,128]{1,0:T(8,128)S(1)}, u32[]{:S(2)}, u32[]{:S(2)}) collective-permute-start(f32[256,128]{1,0:T(8,128)} %bitcast.11), channel_id=1, source_target_pairs={{4,8},{8,4},{12,16},{16,12},{20,24},{24,20},{28,0},{0,28},{5,9},{9... | collective-permute-start | bytes 393224 | tf_op jit(solution)/shard_map/ppermute | solution.py:26
  6.0 0.0 collective-permute-start.7
  6.0 0.7 %collective-permute-start.6 = (f32[256,128]{1,0:T(8,128)}, f32[256,128]{1,0:T(8,128)S(1)}, u32[]{:S(2)}, u32[]{:S(2)}) collective-permute-start(f32[256,128]{1,0:T(8,128)} %bitcast.13), channel_id=1, source_target_pairs={{1,2},{2,1},{3,0},{0,3},{5,6},{6,5},{7,4},{4,7},{9,10},{10,9},{11,... | collective-permute-start | bytes 393224 | tf_op jit(solution)/shard_map/ppermute | solution.py:26
  6.7 1.5 %slice_reduce_fusion = f32[64]{0:T(128)S(1)} fusion(f32[1,1,64,4,128]{4,3,2,1,0:T(4,128)} %param.4), kind=kLoop, calls=%fused_computation | loop fusion | flops 8128 | bytes 33024 | tf_op jit(solution)/shard_map/reduce_sum | solution.py:206
  8.2 0.8 %select_reduce_fusion = f32[16]{0:T(128)S(1)} fusion(f32[64]{0:T(128)S(1)} %slice_reduce_fusion, s32[64]{0:T(128)} %bitcast.17), kind=kLoop, calls=%fused_computation.1 | loop fusion | flops 3056 | bytes 576 | tf_op jit(solution)/shard_map/reduce_sum | solution.py:208
  8.9 1.8 %collective-permute-start = (f32[16]{0:T(128)S(1)}, f32[16]{0:T(128)S(1)}, u32[]{:S(2)}, u32[]{:S(2)}) collective-permute-start(f32[16]{0:T(128)S(1)} %select_reduce_fusion), channel_id=1, source_target_pairs={{0,4},{4,0},{8,12},{12,8},{16,20},{20,16},{24,28},{28,24},{1,5},{5... | collective-permute-start | bytes 200 | tf_op jit(solution)/shard_map/ppermute | solution.py:37
  10.7 1.9 %collective-permute-done = f32[16]{0:T(128)S(1)} collective-permute-done((f32[16]{0:T(128)S(1)}, f32[16]{0:T(128)S(1)}, u32[]{:S(2)}, u32[]{:S(2)}) %collective-permute-start) | collective-permute-done | bytes 96 | tf_op jit(solution)/shard_map/ppermute | solution.py:37
  12.6 0.0 collective-permute-start.1
  12.6 3.5 %collective-permute-done.1 = f32[16]{0:T(128)S(1)} collective-permute-done((f32[16]{0:T(128)S(1)}, f32[16]{0:T(128)S(1)}, u32[]{:S(2)}, u32[]{:S(2)}) %collective-permute-start.1) | collective-permute-done | bytes 96 | tf_op jit(solution)/shard_map/ppermute | solution.py:37
  16.2 0.7 %collective-permute-start.2 = (f32[16]{0:T(128)S(1)}, f32[16]{0:T(128)S(1)}, u32[]{:S(2)}, u32[]{:S(2)}) collective-permute-start(f32[16]{0:T(128)S(1)} %add.25), channel_id=1, source_target_pairs={{0,16},{4,20},{8,24},{12,28},{16,0},{20,4},{24,8},{28,12},{1,17},{... | collective-permute-start | bytes 200 | tf_op jit(solution)/shard_map/ppermute | solution.py:37
  16.9 3.7 %collective-permute-done.2 = f32[16]{0:T(128)S(1)} collective-permute-done((f32[16]{0:T(128)S(1)}, f32[16]{0:T(128)S(1)}, u32[]{:S(2)}, u32[]{:S(2)}) %collective-permute-start.2) | collective-permute-done | bytes 96 | tf_op jit(solution)/shard_map/ppermute | solution.py:37
  20.6 0.0 collective-permute-start.3
  20.6 0.5 %collective-permute-start.5 = (f32[256,128]{1,0:T(8,128)}, f32[256,128]{1,0:T(8,128)S(1)}, u32[]{:S(2)}, u32[]{:S(2)}) collective-permute-start(f32[256,128]{1,0:T(8,128)} %bitcast.14), channel_id=1, source_target_pairs={{0,1},{1,0},{2,3},{3,2},{4,5},{5,4},{6,7},{7,6},{8,9},{9,8},{10,11... | collective-permute-start | bytes 393224 | tf_op jit(solution)/shard_map/ppermute | solution.py:26
  21.1 0.6 %collective-permute-done.3 = f32[16]{0:T(128)S(1)} collective-permute-done((f32[16]{0:T(128)S(1)}, f32[16]{0:T(128)S(1)}, u32[]{:S(2)}, u32[]{:S(2)}) %collective-permute-start.3) | collective-permute-done | bytes 96 | tf_op jit(solution)/shard_map/ppermute | solution.py:37
  21.7 1.5 %collective-permute-start.4 = (f32[16]{0:T(128)S(1)}, f32[16]{0:T(128)S(1)}, u32[]{:S(2)}, u32[]{:S(2)}) collective-permute-start(f32[16]{0:T(128)S(1)} %add.27), channel_id=1, source_target_pairs={{0,2},{1,3},{2,0},{3,1},{4,6},{5,7},{6,4},{7,5},{8,10},{9,11},{10,... | collective-permute-start | bytes 200 | tf_op jit(solution)/shard_map/ppermute | solution.py:37
  23.3 0.0 collective-permute-done.10.refs_6_
  23.3 0.0 collective-permute-start.12
  23.3 2.0 %collective-permute-done.4 = f32[16]{0:T(128)S(1)} collective-permute-done((f32[16]{0:T(128)S(1)}, f32[16]{0:T(128)S(1)}, u32[]{:S(2)}, u32[]{:S(2)}) %collective-permute-start.4) | collective-permute-done | bytes 96 | tf_op jit(solution)/shard_map/ppermute | solution.py:37
  25.3 0.0 collective-permute-start.11
  25.3 0.0 collective-permute-done.7.refs_3_
  25.3 1.6 %collective-permute-start.9 = (f32[256,128]{1,0:T(8,128)S(1)}, f32[256,128]{1,0:T(8,128)S(1)}, u32[]{:S(2)}, u32[]{:S(2)}) collective-permute-start(f32[256,128]{1,0:T(8,128)S(1)} %collective-permute-done.7.refs_3_), channel_id=1, source_target_pairs={{1,2},{2,1},{3,0},{0,3},{5,6},{6,5},{7,4},{4,7},{9,10},{10,9},{11,... | collective-permute-start | bytes 393224 | tf_op jit(solution)/shard_map/ppermute | solution.py:26
  26.9 0.0 collective-permute-done.6.refs_2_
  26.9 0.0 collective-permute-start.8
  27.6 0.8 %copy.7 = s32[1,1,32,16]{3,2,1,0:T(8,128)S(1)} copy(s32[1,1,32,16]{2,3,1,0:T(8,128)} %param.6) | data formatting | bytes 4096 | tf_op args[2]
  28.4 0.1 pad_add_fusion.place
  28.4 0.0 collective-permute-done.5.refs_1_
  28.4 0.5 %collective-permute-done.12.refs_8_ = f32[256,128]{1,0:T(8,128)S(1)} collective-permute-done((f32[256,128]{1,0:T(8,128)S(1)}, f32[256,128]{1,0:T(8,128)S(1)}, u32[]{:S(2)}, u32[]{:S(2)}) %collective-permute-start.12) | collective-permute-done | bytes 131104 | tf_op jit(solution)/shard_map/ppermute | solution.py:26
  29.0 0.0 collective-permute-done.11.refs_7_
  29.0 2.8 %collective-permute-done.9.refs_5_ = f32[256,128]{1,0:T(8,128)S(1)} collective-permute-done((f32[256,128]{1,0:T(8,128)S(1)}, f32[256,128]{1,0:T(8,128)S(1)}, u32[]{:S(2)}, u32[]{:S(2)}) %collective-permute-start.9) | collective-permute-done | bytes 131104 | tf_op jit(solution)/shard_map/ppermute | solution.py:26
  31.8 0.0 collective-permute-done.8.refs_4_
  31.8 16.9 %shard_map.46 = f32[32,3,128]{2,1,0:T(4,128)S(1)} custom-call(s32[4]{0:T(128)S(1)} %pad_add_fusion.place, s32[1]{0:T(128)} %bitcast.9.limit, s32[32,16]{1,0:T(8,128)S(1)} %bitcast.16, f32[16]{0:T(128)S(1)} %add.28.cell_mass, f32[256,128]{1,0:T(8,128)S(1)} %bitcast.15, f32[256,128]{1,0:T(8,128)S(1)} %collective-permute-done.5.refs_1_, ...), custom_call_target="tpu_custom_call" | custom-call | tf_op jit(solution)/shard_map/pallas_call | solution.py:214
  48.6 0.6 %copy.8 = f32[1,1,32,3,128]{4,2,3,1,0:T(8,128)} copy(f32[1,1,32,3,128]{4,3,2,1,0:T(4,128)S(1)} %bitcast.10) | data formatting | bytes 98304 | tf_op jit(solution)/shard_map/broadcast_in_dim | solution.py:228
  (7 shorter events, 0.0 us)
Async XLA Ops:
  0.0 31.8 %copy-start = (f32[1,1,64,4,128]{4,3,2,1,0:T(4,128)S(1)}, f32[1,1,64,4,128]{4,3,2,1,0:T(4,128)}, u32[]{:S(2)}) copy-start(f32[1,1,64,4,128]{4,3,2,1,0:T(4,128)} %param.4) | copy-start | bytes 393220
  0.0 23.3 %collective-permute-start.10 = (f32[256,128]{1,0:T(8,128)}, f32[256,128]{1,0:T(8,128)S(1)}, u32[]{:S(2)}, u32[]{:S(2)}) collective-permute-start(f32[256,128]{1,0:T(8,128)} %bitcast.11), channel_id=1, source_target_pairs={{4,8},{8,4},{12,16},{16,12},{20,24},{24,20},{28,0},{0,28},{5,9},{9... | collective-permute-start | bytes 393224 | tf_op jit(solution)/shard_map/ppermute | solution.py:26
  6.0 19.3 %collective-permute-start.7 = (f32[256,128]{1,0:T(8,128)}, f32[256,128]{1,0:T(8,128)S(1)}, u32[]{:S(2)}, u32[]{:S(2)}) collective-permute-start(f32[256,128]{1,0:T(8,128)} %bitcast.12), channel_id=1, source_target_pairs={{0,4},{4,0},{8,12},{12,8},{16,20},{20,16},{24,28},{28,24},{1,5},{5... | collective-permute-start | bytes 393224 | tf_op jit(solution)/shard_map/ppermute | solution.py:26
  6.0 20.9 %collective-permute-start.6 = (f32[256,128]{1,0:T(8,128)}, f32[256,128]{1,0:T(8,128)S(1)}, u32[]{:S(2)}, u32[]{:S(2)}) collective-permute-start(f32[256,128]{1,0:T(8,128)} %bitcast.13), channel_id=1, source_target_pairs={{1,2},{2,1},{3,0},{0,3},{5,6},{6,5},{7,4},{4,7},{9,10},{10,9},{11,... | collective-permute-start | bytes 393224 | tf_op jit(solution)/shard_map/ppermute | solution.py:26
  8.9 3.7 %collective-permute-start = (f32[16]{0:T(128)S(1)}, f32[16]{0:T(128)S(1)}, u32[]{:S(2)}, u32[]{:S(2)}) collective-permute-start(f32[16]{0:T(128)S(1)} %select_reduce_fusion), channel_id=1, source_target_pairs={{0,4},{4,0},{8,12},{12,8},{16,20},{20,16},{24,28},{28,24},{1,5},{5... | collective-permute-start | bytes 200 | tf_op jit(solution)/shard_map/ppermute | solution.py:37
  12.6 3.5 %collective-permute-start.1 = (f32[16]{0:T(128)S(1)}, f32[16]{0:T(128)S(1)}, u32[]{:S(2)}, u32[]{:S(2)}) collective-permute-start(f32[16]{0:T(128)S(1)} %add.24), channel_id=1, source_target_pairs={{0,8},{4,12},{8,0},{12,4},{16,24},{20,28},{24,16},{28,20},{1,9},{5... | collective-permute-start | bytes 200 | tf_op jit(solution)/shard_map/ppermute | solution.py:37
  16.2 4.4 %collective-permute-start.2 = (f32[16]{0:T(128)S(1)}, f32[16]{0:T(128)S(1)}, u32[]{:S(2)}, u32[]{:S(2)}) collective-permute-start(f32[16]{0:T(128)S(1)} %add.25), channel_id=1, source_target_pairs={{0,16},{4,20},{8,24},{12,28},{16,0},{20,4},{24,8},{28,12},{1,17},{... | collective-permute-start | bytes 200 | tf_op jit(solution)/shard_map/ppermute | solution.py:37
  20.6 1.1 %collective-permute-start.3 = (f32[16]{0:T(128)S(1)}, f32[16]{0:T(128)S(1)}, u32[]{:S(2)}, u32[]{:S(2)}) collective-permute-start(f32[16]{0:T(128)S(1)} %add.26), channel_id=1, source_target_pairs={{0,1},{1,0},{2,3},{3,2},{4,5},{5,4},{6,7},{7,6},{8,9},{9,8},{10,11... | collective-permute-start | bytes 200 | tf_op jit(solution)/shard_map/ppermute | solution.py:37
  20.6 7.8 %collective-permute-start.5 = (f32[256,128]{1,0:T(8,128)}, f32[256,128]{1,0:T(8,128)S(1)}, u32[]{:S(2)}, u32[]{:S(2)}) collective-permute-start(f32[256,128]{1,0:T(8,128)} %bitcast.14), channel_id=1, source_target_pairs={{0,1},{1,0},{2,3},{3,2},{4,5},{5,4},{6,7},{7,6},{8,9},{9,8},{10,11... | collective-permute-start | bytes 393224 | tf_op jit(solution)/shard_map/ppermute | solution.py:26
  21.7 3.5 %collective-permute-start.4 = (f32[16]{0:T(128)S(1)}, f32[16]{0:T(128)S(1)}, u32[]{:S(2)}, u32[]{:S(2)}) collective-permute-start(f32[16]{0:T(128)S(1)} %add.27), channel_id=1, source_target_pairs={{0,2},{1,3},{2,0},{3,1},{4,6},{5,7},{6,4},{7,5},{8,10},{9,11},{10,... | collective-permute-start | bytes 200 | tf_op jit(solution)/shard_map/ppermute | solution.py:37
  23.3 5.7 %collective-permute-start.12 = (f32[256,128]{1,0:T(8,128)S(1)}, f32[256,128]{1,0:T(8,128)S(1)}, u32[]{:S(2)}, u32[]{:S(2)}) collective-permute-start(f32[256,128]{1,0:T(8,128)S(1)} %collective-permute-done.10.refs_6_), channel_id=1, source_target_pairs={{1,2},{2,1},{3,0},{0,3},{5,6},{6,5},{7,4},{4,7},{9,10},{10,9},{11,... | collective-permute-start | bytes 393224 | tf_op jit(solution)/shard_map/ppermute | solution.py:26
  25.3 3.7 %collective-permute-start.11 = (f32[256,128]{1,0:T(8,128)S(1)}, f32[256,128]{1,0:T(8,128)S(1)}, u32[]{:S(2)}, u32[]{:S(2)}) collective-permute-start(f32[256,128]{1,0:T(8,128)S(1)} %collective-permute-done.10.refs_6_), channel_id=1, source_target_pairs={{0,1},{1,0},{2,3},{3,2},{4,5},{5,4},{6,7},{7,6},{8,9},{9,8},{10,11... | collective-permute-start | bytes 393224 | tf_op jit(solution)/shard_map/ppermute | solution.py:26
  25.3 6.5 %collective-permute-start.9 = (f32[256,128]{1,0:T(8,128)S(1)}, f32[256,128]{1,0:T(8,128)S(1)}, u32[]{:S(2)}, u32[]{:S(2)}) collective-permute-start(f32[256,128]{1,0:T(8,128)S(1)} %collective-permute-done.7.refs_3_), channel_id=1, source_target_pairs={{1,2},{2,1},{3,0},{0,3},{5,6},{6,5},{7,4},{4,7},{9,10},{10,9},{11,... | collective-permute-start | bytes 393224 | tf_op jit(solution)/shard_map/ppermute | solution.py:26
  26.9 4.8 %collective-permute-start.8 = (f32[256,128]{1,0:T(8,128)S(1)}, f32[256,128]{1,0:T(8,128)S(1)}, u32[]{:S(2)}, u32[]{:S(2)}) collective-permute-start(f32[256,128]{1,0:T(8,128)S(1)} %collective-permute-done.7.refs_3_), channel_id=1, source_target_pairs={{0,1},{1,0},{2,3},{3,2},{4,5},{5,4},{6,7},{7,6},{8,9},{9,8},{10,11... | collective-permute-start | bytes 393224 | tf_op jit(solution)/shard_map/ppermute | solution.py:26
